TPU v7x, 32 devices: a whole 2x2x4 slice. The times are simulated.
32 devices in a mesh: members: 2 (over x), wave: 16 (over z, y, core).
Axes of the slice: x: 2, y: 2, z: 4, core: 2. Of those that a mesh axis runs over, the one named last changes fastest.
Arguments:
- grid_grad: bfloat16 [64, 640, 2560], P('members', 'wave'), parts along dimension 0, may hold values from -6 to 6
- legendre: bfloat16 [640, 1280, 320], P('wave'), may hold values from -0.25 to 0.25
- spectrum: float32 [1280], replicated, may hold values from 0.25 to 4
- owner_waves: int32 [640], replicated, may hold values from 0 to 639, each once
- lat_order: int32 [640], replicated, may hold values from 0 to 639, each once
Outputs:
- gradient_spectra: bfloat16 [1280, 64, 1280], P(('members', 'wave')), parts along dimension 0
- smoothed_grid: bfloat16 [64, 640, 2560], P('members', 'wave'), parts along dimension 0
There are 2 independent parts, one for each index of `members`. A program takes and returns all parts, laid end to end along the dimension named above; an argument that names none is the same for every part. Nothing has to cross between parts.
Inputs may be any that keep to these rules, and one draw needn't show every extreme that they name: `owner_waves`: each zonal wavenumber is held by exactly one slot; a device along wave holds 640 / 16 consecutive slots. `lat_order`: each latitude is held by exactly one stored row; latitude j < 320 is northern row j and latitude 320 + j is its southern mirror.
All inputs are finite; a program needn't handle non-finite values.
Results may differ from a plain program's by a relative error of at most 0.015.
Values may be sent and summed in bfloat16 or wider, within the bound.
A program may use at most 256 MiB of HBM per device.

v0:
```python
import functools
import math

import jax
import jax.numpy as jnp
from jax import lax
from jax.experimental import pallas as pl
from jax.experimental.pallas import tpu as pltpu
from jax.sharding import PartitionSpec as P

LANES = 128
PARTS = 4
VMEM = 56 * 2**20
F32 = jnp.float32
BF16 = jnp.bfloat16


def up(value, step):
    return -(-value // step) * step


def params(**extra):
    return pltpu.CompilerParams(vmem_limit_bytes=VMEM, **extra)


def angle_tables(waves, lon_cells):
    chunks, owners, slots = waves.shape
    quarter = lon_cells // 4
    coarse_count = lon_cells // LANES
    rows = jnp.broadcast_to(waves[:, :, None, :], (chunks, owners, 2, slots)).reshape(-1, 1)
    turn = jnp.arange(2, dtype=jnp.int32)[None, None, :, None] * quarter
    turn = jnp.broadcast_to(turn, (chunks, owners, 2, slots)).reshape(-1, 1)
    fine = rows * jnp.arange(LANES, dtype=jnp.int32)
    coarse = rows * (jnp.arange(coarse_count, dtype=jnp.int32) * LANES) + turn
    ticks = jnp.concatenate([fine, fine + 3 * quarter, coarse, coarse + 3 * quarter], axis=1) % lon_cells
    return jnp.cos(ticks.astype(F32) * (2.0 * math.pi / lon_cells))


def exchange_body(
    owners, chunks, wave_ref, x_hbm, angles_ref, place_ref, leg_hbm, spectrum_ref,
    spec_hbm, returned_hbm, table_hbm,
    x_ref, table_ref, y_ref, sent, recv, back, side, fold, leg_buf, spec_buf,
    fsend, frecv, bsend, brecv, load_sem, leg_sem, spec_sem, own_sem,
):
    slots, north, total = leg_hbm.shape
    lon_cells = x_hbm.shape[1]
    chunk = slots // chunks
    piece = 2 * chunk
    rows_dev = sent.shape[2]
    lanes = sent.shape[3]
    levels = lanes // piece
    items = lanes // chunk
    columns = owners * piece
    lat_rows = owners * rows_dev
    blocks = side.shape[0]
    half = blocks // 2
    buffers = leg_buf.shape[0]
    me = lax.axis_index("wave")

    load_x = pltpu.make_async_copy(x_hbm, x_ref, load_sem.at[0])
    load_x.start()

    def leg_copy(g):
        slot = lax.rem(g, buffers)
        return pltpu.make_async_copy(leg_hbm.at[g], leg_buf.at[slot], leg_sem.at[slot])

    def spec_copy(g):
        slot = lax.rem(g, 2)
        return pltpu.make_async_copy(spec_buf.at[slot], spec_hbm.at[g], spec_sem.at[slot])

    def out_copy(h, d):
        target = lax.rem(me + d, owners)
        return pltpu.make_async_remote_copy(
            src_ref=sent.at[h, target], dst_ref=recv.at[h, me],
            send_sem=fsend.at[h, d], recv_sem=frecv.at[h, d],
            device_id={"wave": target}, device_id_type=pl.DeviceIdType.MESH,
        )

    def in_copy(h, d):
        source = lax.rem(me + owners - d, owners)
        return pltpu.make_async_remote_copy(
            src_ref=sent.at[h, source], dst_ref=recv.at[h, source],
            send_sem=fsend.at[h, d], recv_sem=frecv.at[h, d],
            device_id={"wave": source}, device_id_type=pl.DeviceIdType.MESH,
        )

    def out_back(h, d):
        target = lax.rem(me + d, owners)
        return pltpu.make_async_remote_copy(
            src_ref=back.at[h, target], dst_ref=returned_hbm.at[h, me],
            send_sem=bsend.at[h, d], recv_sem=brecv.at[h, d],
            device_id={"wave": target}, device_id_type=pl.DeviceIdType.MESH,
        )

    def in_back(h, d):
        source = lax.rem(me + owners - d, owners)
        return pltpu.make_async_remote_copy(
            src_ref=back.at[h, source], dst_ref=returned_hbm.at[h, source],
            send_sem=bsend.at[h, d], recv_sem=brecv.at[h, d],
            device_id={"wave": source}, device_id_type=pl.DeviceIdType.MESH,
        )

    def own_back(h):
        return pltpu.make_async_copy(back.at[h, me], returned_hbm.at[h, me], own_sem.at[h])

    def loop(low, high, step):
        def body(i, carry):
            step(i)
            return carry

        lax.fori_loop(low, high, body, 0)

    barrier = pltpu.get_barrier_semaphore()

    def greet(d):
        pl.semaphore_signal(
            barrier, inc=1, device_id={"wave": lax.rem(me + d, owners)}, device_id_type=pl.DeviceIdType.MESH
        )

    loop(1, owners, greet)
    for g in range(buffers - 1):
        leg_copy(g).start()

    coarse = lon_cells // LANES

    def table_chunk(h):
        def rows_step(t):
            rows = pl.ds(pl.multiple_of(h * columns + t * 16, 16), 16)
            local = pl.ds(pl.multiple_of(t * 16, 16), 16)
            cos_lo = angles_ref[rows, 0:LANES]
            sin_lo = angles_ref[rows, LANES : 2 * LANES]
            high = angles_ref[rows, 2 * LANES : 2 * LANES + 2 * coarse]
            for b in range(coarse):
                value = high[:, b : b + 1] * cos_lo - high[:, coarse + b : coarse + b + 1] * sin_lo
                table_ref[h, local, b * LANES : (b + 1) * LANES] = value.astype(BF16)

        loop(0, columns // 16, rows_step)

    factor = 1.0 / math.sqrt(lon_cells)
    tile = 4 * rows_dev * 2

    def forward_chunk(h):
        table_chunk(h)

        @pl.when(h == 0)
        def _():
            load_x.wait()

        def dot_step(t):
            rows = pl.ds(pl.multiple_of(t * tile, tile), tile)
            y_ref[rows, :] = lax.dot_general(
                x_ref[rows, :], table_ref[h], (((1,), (1,)), ((), ())), preferred_element_type=F32
            ) * factor

        loop(0, levels * rows_dev // tile, dot_step)
        for w in range(owners):
            parts = [
                y_ref[k * rows_dev : (k + 1) * rows_dev, w * piece : (w + 1) * piece] for k in range(levels)
            ]
            sent[h, w] = jnp.concatenate(parts, axis=1).astype(BF16)

        @pl.when(h == 0)
        def _():
            pl.semaphore_wait(barrier, owners - 1)

        loop(1, owners, lambda d: out_copy(h, d).start())
        recv[h, me] = sent[h, me]

    loop(0, chunks, forward_chunk)
    save_table = pltpu.make_async_copy(table_ref, table_hbm, load_sem.at[1])
    save_table.start()

    wide = 128

    def middle_chunk(h):
        loop(1, owners, lambda d: in_copy(h, d).wait_recv())

        def unpack(t):
            cols = pl.ds(pl.multiple_of(t * wide, wide), wide)
            rows = recv[h, :, :, cols].astype(F32).reshape(lat_rows, wide).astype(BF16)
            value = lax.dot_general(
                rows, place_ref[...], (((0,), (0,)), ((), ())), preferred_element_type=F32
            )
            for b in range(blocks):
                side[b, cols, :] = value[:, b * LANES : (b + 1) * LANES]

        loop(0, lanes // wide, unpack)

        def slot_step(s):
            g = h * chunk + s

            @pl.when(g + buffers - 1 < slots)
            def _():
                leg_copy(g + buffers - 1).start()

            mine = pl.ds(s, items, stride=chunk)
            upper = jnp.concatenate([side[b, mine, :] for b in range(half)], axis=1)
            lower = jnp.concatenate([side[b, mine, :] for b in range(half, blocks)], axis=1)
            both = jnp.concatenate([upper, lower], axis=0)[:, :north].astype(BF16)
            leg_copy(g).wait()
            table = leg_buf[lax.rem(g, buffers)]
            result = jnp.dot(both, table, preferred_element_type=F32)
            offsets = lax.broadcasted_iota(jnp.int32, (1, total), 1) - wave_ref[g]
            sign = jnp.where(offsets % 2 == 0, 1.0, -1.0).astype(F32)
            spec = jnp.where(offsets >= 0, result[:items] + sign * result[items:], 0.0)

            @pl.when(g >= 2)
            def _():
                spec_copy(g - 2).wait()

            spec_buf[lax.rem(g, 2)] = spec.astype(BF16)
            spec_copy(g).start()
            filtered = (spec * spectrum_ref[...]).astype(BF16).astype(F32)
            second = jnp.concatenate([filtered, filtered * sign], axis=0).astype(BF16)
            folded = lax.dot_general(second, table, (((1,), (1,)), ((), ())), preferred_element_type=F32)
            folded = folded.astype(BF16).astype(F32)
            if half * LANES > north:
                pad = jnp.zeros((2 * items, half * LANES - north), F32)
                folded = jnp.concatenate([folded, pad], axis=1)
            for b in range(half):
                part = slice(b * LANES, (b + 1) * LANES)
                fold[b, mine, :] = folded[:items, part]
                fold[half + b, mine, :] = folded[items:, part]

        loop(0, chunk, slot_step)

        def pack(t):
            cols = pl.ds(pl.multiple_of(t * wide, wide), wide)
            value = jnp.concatenate([fold[b, cols, :] for b in range(blocks)], axis=1).astype(BF16)
            rows = lax.dot_general(
                place_ref[...], value, (((1,), (1,)), ((), ())), preferred_element_type=F32
            )
            back[h, :, :, cols] = rows.reshape(owners, rows_dev, wide).astype(BF16)

        loop(0, lanes // wide, pack)
        loop(1, owners, lambda d: out_back(h, d).start())
        own_back(h).start()

    loop(0, chunks, middle_chunk)
    spec_copy(slots - 2).wait()
    spec_copy(slots - 1).wait()
    save_table.wait()

    def finish(h):
        loop(1, owners, lambda d: out_copy(h, d).wait_send())
        loop(1, owners, lambda d: out_back(h, d).wait_send())
        loop(1, owners, lambda d: in_back(h, d).wait_recv())
        own_back(h).wait()

    loop(0, chunks, finish)


def exchange(chunks, owners, rows_dev, mine, x, angles, place, table, spectrum):
    slots, north, total = table.shape
    lon_cells = x.shape[1]
    levels = x.shape[0] // rows_dev
    chunk = slots // chunks
    lanes = 2 * levels * chunk
    columns = owners * 2 * chunk
    blocks = place.shape[1] // LANES
    hbm = pl.BlockSpec(memory_space=pl.ANY)
    vmem = pl.BlockSpec(memory_space=pltpu.VMEM)
    block = (chunks, owners, rows_dev, lanes)
    sems = pltpu.SemaphoreType.DMA
    return pl.pallas_call(
        functools.partial(exchange_body, owners, chunks),
        in_specs=[pl.BlockSpec(memory_space=pltpu.SMEM), hbm, vmem, vmem, hbm, vmem],
        out_specs=[hbm, hbm, hbm],
        out_shape=[
            jax.ShapeDtypeStruct((slots, 2 * levels, total), BF16),
            jax.ShapeDtypeStruct(block, BF16),
            jax.ShapeDtypeStruct((chunks, columns, lon_cells), BF16),
        ],
        scratch_shapes=[
            pltpu.VMEM(x.shape, BF16),
            pltpu.VMEM((chunks, columns, lon_cells), BF16),
            pltpu.VMEM((x.shape[0], columns), F32),
            pltpu.VMEM(block, BF16),
            pltpu.VMEM(block, BF16),
            pltpu.VMEM(block, BF16),
            pltpu.VMEM((blocks, lanes, LANES), F32),
            pltpu.VMEM((blocks, lanes, LANES), F32),
            pltpu.VMEM((4, north, total), BF16),
            pltpu.VMEM((2, 2 * levels, total), BF16),
            sems((chunks, owners)),
            sems((chunks, owners)),
            sems((chunks, owners)),
            sems((chunks, owners)),
            sems((2,)),
            sems((4,)),
            sems((2,)),
            sems((chunks,)),
        ],
        compiler_params=params(collective_id=0, has_side_effects=True),
        cost_estimate=pl.CostEstimate(
            flops=2 * x.size * columns * chunks + 8 * slots * north * total * 2 * levels,
            bytes_accessed=2 * (x.size + table.size) + 8 * x.size,
            transcendentals=0,
        ),
        name="fourier_legendre_exchange",
    )(mine, x, angles, place, table, spectrum)


def inverse_body(rows_dev, group, piece, factor, returned_ref, table_ref, out_ref):
    chunks, owners = returned_ref.shape[:2]
    total = None
    for h in range(chunks):
        blocks = [returned_ref[h, w].astype(F32) for w in range(owners)]
        rows = [
            jnp.concatenate([b[:, k * piece : (k + 1) * piece] for b in blocks], axis=1)
            for k in range(group)
        ]
        z = jnp.concatenate(rows, axis=0).astype(BF16)
        term = jnp.dot(z, table_ref[h], preferred_element_type=F32)
        total = term if total is None else total + term
    out_ref[...] = (total * factor).astype(BF16)


def inverse(returned, tables, waves_count):
    chunks, owners, rows_dev, lanes = returned.shape
    columns, lon_cells = tables.shape[1:]
    piece = columns // owners
    items = lanes // piece
    group = LANES // math.gcd(piece, LANES)
    body = functools.partial(inverse_body, rows_dev, group, piece, 1.0 / math.sqrt(waves_count))
    return pl.pallas_call(
        body,
        grid=(items // group,),
        in_specs=[
            pl.BlockSpec((chunks, owners, rows_dev, group * piece), lambda g: (0, 0, 0, g)),
            pl.BlockSpec(tables.shape, lambda g: (0, 0, 0)),
        ],
        out_specs=pl.BlockSpec((group * rows_dev, lon_cells), lambda g: (g, 0)),
        out_shape=jax.ShapeDtypeStruct((items * rows_dev, lon_cells), BF16),
        compiler_params=params(),
        name="inverse_fourier",
    )(returned, tables)


def kernels_fit(owners, items, rows_dev, slots, north, total, lon_cells):
    chunk = slots // PARTS
    piece = 2 * chunk
    group = LANES // math.gcd(piece, LANES)
    return (
        slots % PARTS == 0
        and rows_dev % 8 == 0
        and items % 8 == 0
        and items % group == 0
        and total % LANES == 0
        and lon_cells % (4 * LANES) == 0
        and owners * piece % 16 == 0
        and slots > 4
    )


def local_kernels(grid_grad, legendre, spectrum, owner_waves, lat_order):
    owners = lax.axis_size("wave")
    items, rows_dev, lon_cells = grid_grad.shape
    slots, total, north = legendre.shape
    waves = owner_waves.reshape(owners, slots)
    mine = lax.dynamic_index_in_dim(waves, lax.axis_index("wave"), 0, keepdims=False)
    x = grid_grad.reshape(items * rows_dev, lon_cells)
    table = jnp.swapaxes(legendre, 1, 2)
    half = up(north, LANES)
    column = jnp.where(lat_order < north, lat_order, lat_order - north + half)
    place = (column[:, None] == lax.iota(jnp.int32, 2 * half)[None, :]).astype(BF16)
    in_chunks = jnp.swapaxes(waves.reshape(owners, PARTS, slots // PARTS), 0, 1)
    angles = angle_tables(in_chunks, lon_cells)
    spec, returned, phases = exchange(
        PARTS, owners, rows_dev, mine, x, angles, place, table, spectrum[None, :]
    )
    smoothed = inverse(returned, phases, owners * slots)
    return (spec, smoothed.reshape(grid_grad.shape))


def phase_table(waves, lon_cells, factor):
    ticks = lax.iota(jnp.int32, lon_cells)
    turns = waves[..., None] * ticks % lon_cells
    angle = turns.astype(jnp.float32) * (2.0 * math.pi / lon_cells)
    return jnp.stack([jnp.cos(angle), -jnp.sin(angle)], axis=1) * factor


def split_table(table):
    high_part = table.astype(jnp.bfloat16)
    low_part = (table - high_part.astype(jnp.float32)).astype(jnp.bfloat16)
    return (high_part, low_part)


def row_signs(count, wave):
    offsets = lax.iota(jnp.int32, count) - wave[..., None]
    return ((1 - 2 * (offsets % 2)).astype(jnp.float32), offsets >= 0)


def legendre_padded(legendre, side, spectrum, mine):
    half = side.shape[2] // 2
    result = jnp.einsum("snj,sjc->scn", legendre, side, preferred_element_type=jnp.float32)
    sign, valid = row_signs(legendre.shape[1], mine)
    spec = jnp.where(valid[:, None, :], result[:, :half] + sign[:, None, :] * result[:, half:], 0.0)
    filtered = (spec * spectrum).astype(jnp.bfloat16)
    second = jnp.concatenate([filtered, filtered * sign[:, None, :].astype(jnp.bfloat16)], axis=1)
    folded = jnp.einsum("snj,scn->scj", legendre, second, preferred_element_type=jnp.float32)
    return (spec, folded)


def local_plain(grid_grad, legendre, spectrum, owner_waves, lat_order):
    owners = lax.axis_size("wave")
    fields_levels, rows_dev, lon_cells = grid_grad.shape
    slots, total_rows, north_rows = legendre.shape
    lat_rows = rows_dev * owners
    waves = owner_waves.reshape(owners, slots)
    mine = lax.dynamic_index_in_dim(waves, lax.axis_index("wave"), 0, keepdims=False)
    forward_high, forward_low = split_table(
        phase_table(waves, lon_cells, 1.0 / math.sqrt(lon_cells))
    )
    inverse_high, inverse_low = split_table(
        phase_table(waves, lon_cells, 1.0 / math.sqrt(owners * slots))
    )
    onehot = (lat_order[None, :] == lax.iota(jnp.int32, lat_rows)[:, None]).astype(jnp.bfloat16)
    onehot = onehot.reshape(2, north_rows, owners, rows_dev)
    fourier = jnp.einsum(
        "kri,wpsi->wkrps", grid_grad, forward_high, preferred_element_type=jnp.float32
    )
    fourier = fourier + jnp.einsum(
        "kri,wpsi->wkrps", grid_grad, forward_low, preferred_element_type=jnp.float32
    )
    fourier = fourier.astype(jnp.bfloat16).reshape(owners, fields_levels, rows_dev, 2 * slots)
    received = lax.all_to_all(fourier, "wave", split_axis=0, concat_axis=0, tiled=True)
    items = received.shape[1]
    split = received.reshape(owners, items, rows_dev, 2, slots)
    side = jnp.einsum("hjwr,wkrps->sjhkp", onehot, split, preferred_element_type=jnp.float32)
    side = side.astype(jnp.bfloat16).reshape(slots, north_rows, 4 * items)
    spec, folded = legendre_padded(legendre, side, spectrum, mine)
    folded = folded.astype(jnp.bfloat16).reshape(slots, 2, items, 2, north_rows)
    back = jnp.einsum("hjwr,shkpj->wkrps", onehot, folded, preferred_element_type=jnp.float32)
    back = back.astype(jnp.bfloat16).reshape(owners, items, rows_dev, 2 * slots)
    returned = lax.all_to_all(back, "wave", split_axis=0, concat_axis=0, tiled=True)
    spec_out = spec.reshape(slots, items, 2, total_rows).astype(jnp.bfloat16)
    spec_out, returned = (spec_out, returned)
    gradient_spectra = spec_out.reshape(slots, 2 * fields_levels, total_rows)
    returned = returned.reshape(owners, fields_levels, rows_dev, 2, slots)
    smoothed = jnp.einsum(
        "wkrps,wpsi->kri", returned, inverse_high, preferred_element_type=jnp.float32
    )
    smoothed = smoothed + jnp.einsum(
        "wkrps,wpsi->kri", returned, inverse_low, preferred_element_type=jnp.float32
    )
    return (gradient_spectra, smoothed.astype(jnp.bfloat16))


def local(grid_grad, legendre, spectrum, owner_waves, lat_order):
    slots, total, north = legendre.shape
    if kernels_fit(lax.axis_size("wave"), *grid_grad.shape[:2], slots, north, total, grid_grad.shape[2]):
        return local_kernels(grid_grad, legendre, spectrum, owner_waves, lat_order)
    return local_plain(grid_grad, legendre, spectrum, owner_waves, lat_order)


def solution(mesh):
    in_specs = (P("members", "wave", None), P("wave", None, None), P(), P(), P())
    out_specs = (P(("members", "wave"), None, None), P("members", "wave", None))
    return jax.shard_map(local, mesh=mesh, in_specs=in_specs, out_specs=out_specs, check_vma=False)
```

profile of v0, /device:TPU:15, one launch (start us, length us, event | category | flops | bytes accessed | tf_op | source)
XLA Modules:
  0.0 197.6 jit_solution(12603196561236218842)
XLA Ops:
  0.7 0.7 compare_select_fusion
  1.3 1.3 broadcast_in_dim.8.spectrum_ref
  2.6 0.8 reshape.28
  3.4 0.5 dynamic-slice_bitcast_fusion.wave_ref
  3.9 0.8 reshape_reshape.3
  4.8 0.1 mul.49
  4.9 0.1 broadcast_in_dim.7
  5.0 0.1 add.44
  5.2 1.2 fusion.3.place_ref
  6.3 0.4 multiply_add_fusion
  6.7 0.2 iota_multiply_fusion
  7.0 8.8 %fusion.2.angles_ref = f32[1280,296]{1,0:T(8,128)} fusion(s32[1280,20]{1,0:T(8,128)S(1)} %get-tuple-element.9, s32[1280,20]{1,0:T(8,128)S(1)} %get-tuple-element.8, s32[1280,128]{1,0:T(8,128)S(1)} %get-tuple-element.11, s32[1280,128]{1,0:T(8,128)S(1)} %get-tuple-element.10), kind=kLoop, calls=%fused_computation.3 | loop fusion | flops 4167680 | bytes 3031040 | tf_op jit(solution)/shard_map/cos | solution.py:36
  15.8 157.4 %fourier_legendre_exchange.1 = (bf16[40,64,1280]{2,1,0:T(8,128)(2,1)}, bf16[4,16,40,640]{3,2,1,0:T(8,128)(2,1)}, bf16[4,320,2560]{2,1,0:T(8,128)(2,1)}) custom-call(s32[40]{0:T(128)} %dynamic-slice_bitcast_fusion.wave_ref, bf16[1280,2560]{1,0:T(8,128)(2,1)} %bitcast.9, f32[1280,296]{1,0:T(8,128)} %fusion.2.angles_ref, bf16[640,768]{1,0:T(8,128)(2,1)} %fusion.3.place_ref, ...), custom_call_target="tpu_custom_call" | custom-call | flops 16777216000 | bytes 65536000 | tf_op jit(solution)/shard_map/fourier_legendre_exchange/pallas_call | solution.py:265
  173.3 0.0 copy-start
  173.3 21.6 %inverse_fourier.1 = bf16[1280,2560]{1,0:T(8,128)(2,1)} custom-call(bf16[4,16,40,640]{3,2,1,0:T(8,128)(2,1)} %get-tuple-element.6.returned_ref, bf16[4,320,2560]{2,1,0:T(8,128)(2,1)} %get-tuple-element.7.table_ref), custom_call_target="tpu_custom_call" | custom-call | tf_op jit(solution)/shard_map/inverse_fourier/pallas_call | solution.py:326
  194.8 0.0 copy-done
  194.8 2.8 %copy.12 = bf16[40,64,1280]{2,1,0:T(8,128)(2,1)} copy(bf16[40,64,1280]{2,1,0:T(8,128)(2,1)S(1)} %copy-done) | data formatting | bytes 13107200
  (4 shorter events, 0.0 us)
Async XLA Ops:
  173.3 21.6 %copy-start = (bf16[40,64,1280]{2,1,0:T(8,128)(2,1)S(1)}, bf16[40,64,1280]{2,1,0:T(8,128)(2,1)}, u32[]{:S(2)}) copy-start(bf16[40,64,1280]{2,1,0:T(8,128)(2,1)} %get-tuple-element.14) | copy-start | bytes 19660804
where the time goes:
time: 198 us
  Pallas kernels  179 us (90%)
  other arithmetic  11.3 us (6%)
  local copies, waits for them, and re-layouts  6.57 us (3%)
    pallas_call x1, Pallas kernels, exchange(): pl.pallas_call(functools.partial(exchange_body, owners, chunks), in_specs...  157 us
    pallas_call x1, Pallas kernels, inverse(): pl.pallas_call(body, grid=(items // group,), in_specs=[pl.BlockSpec((chun...  21.6 us
    cos x1, other arithmetic, angle_tables(): return jnp.cos(ticks.astype(F32) * (2.0 * math.pi / lon_cells))  8.83 us

commit v1 on v0

--- a/solution.py
+++ b/solution.py
@@ -2,6 +2,8 @@
 import math
 
 import jax
+import ml_dtypes
+import numpy as np
 import jax.numpy as jnp
 from jax import lax
 from jax.experimental import pallas as pl
@@ -10,7 +12,7 @@
 
 LANES = 128
 PARTS = 4
-VMEM = 56 * 2**20
+VMEM = 62 * 2**20
 F32 = jnp.float32
 BF16 = jnp.bfloat16
 
@@ -23,24 +25,18 @@
     return pltpu.CompilerParams(vmem_limit_bytes=VMEM, **extra)
 
 
-def angle_tables(waves, lon_cells):
-    chunks, owners, slots = waves.shape
-    quarter = lon_cells // 4
-    coarse_count = lon_cells // LANES
-    rows = jnp.broadcast_to(waves[:, :, None, :], (chunks, owners, 2, slots)).reshape(-1, 1)
-    turn = jnp.arange(2, dtype=jnp.int32)[None, None, :, None] * quarter
-    turn = jnp.broadcast_to(turn, (chunks, owners, 2, slots)).reshape(-1, 1)
-    fine = rows * jnp.arange(LANES, dtype=jnp.int32)
-    coarse = rows * (jnp.arange(coarse_count, dtype=jnp.int32) * LANES) + turn
-    ticks = jnp.concatenate([fine, fine + 3 * quarter, coarse, coarse + 3 * quarter], axis=1) % lon_cells
-    return jnp.cos(ticks.astype(F32) * (2.0 * math.pi / lon_cells))
+def phase_constants(count, lon_cells):
+    turns = np.arange(count)[:, None] * np.arange(lon_cells)[None, :] % lon_cells
+    angle = turns * (2.0 * np.pi / lon_cells)
+    return np.concatenate([np.cos(angle), -np.sin(angle)], axis=0).astype(ml_dtypes.bfloat16)
 
 
 def exchange_body(
-    owners, chunks, wave_ref, x_hbm, angles_ref, place_ref, leg_hbm, spectrum_ref,
-    spec_hbm, returned_hbm, table_hbm,
-    x_ref, table_ref, y_ref, sent, recv, back, side, fold, leg_buf, spec_buf,
-    fsend, frecv, bsend, brecv, load_sem, leg_sem, spec_sem, own_sem,
+    owners, chunks, wave_ref, x_hbm, phase_hbm, pick_ref, column_ref, leg_hbm, spectrum_ref,
+    spec_hbm, smooth_hbm,
+    x_ref, phase_ref, table_ref, y_ref, total_ref, place_ref,
+    sent, recv, back, returned, side, fold, leg_buf, spec_buf,
+    fsend, frecv, bsend, brecv, load_sem, leg_sem, spec_sem, smooth_sem,
 ):
     slots, north, total = leg_hbm.shape
     lon_cells = x_hbm.shape[1]
@@ -58,6 +54,8 @@
     me = lax.axis_index("wave")
 
     load_x = pltpu.make_async_copy(x_hbm, x_ref, load_sem.at[0])
+    load_phase = pltpu.make_async_copy(phase_hbm, phase_ref, load_sem.at[1])
+    load_phase.start()
     load_x.start()
 
     def leg_copy(g):
@@ -87,7 +85,7 @@
     def out_back(h, d):
         target = lax.rem(me + d, owners)
         return pltpu.make_async_remote_copy(
-            src_ref=back.at[h, target], dst_ref=returned_hbm.at[h, me],
+            src_ref=back.at[h, target], dst_ref=returned.at[h, me],
             send_sem=bsend.at[h, d], recv_sem=brecv.at[h, d],
             device_id={"wave": target}, device_id_type=pl.DeviceIdType.MESH,
         )
@@ -95,13 +93,10 @@
     def in_back(h, d):
         source = lax.rem(me + owners - d, owners)
         return pltpu.make_async_remote_copy(
-            src_ref=back.at[h, source], dst_ref=returned_hbm.at[h, source],
+            src_ref=back.at[h, source], dst_ref=returned.at[h, source],
             send_sem=bsend.at[h, d], recv_sem=brecv.at[h, d],
             device_id={"wave": source}, device_id_type=pl.DeviceIdType.MESH,
         )
-
-    def own_back(h):
-        return pltpu.make_async_copy(back.at[h, me], returned_hbm.at[h, me], own_sem.at[h])
 
     def loop(low, high, step):
         def body(i, carry):
@@ -121,20 +116,22 @@
     for g in range(buffers - 1):
         leg_copy(g).start()
 
-    coarse = lon_cells // LANES
+    place_ref[...] = jnp.where(
+        lax.broadcasted_iota(jnp.int32, place_ref.shape, 0) == column_ref[...], 1.0, 0.0
+    ).astype(BF16)
+    load_phase.wait()
 
     def table_chunk(h):
-        def rows_step(t):
-            rows = pl.ds(pl.multiple_of(h * columns + t * 16, 16), 16)
-            local = pl.ds(pl.multiple_of(t * 16, 16), 16)
-            cos_lo = angles_ref[rows, 0:LANES]
-            sin_lo = angles_ref[rows, LANES : 2 * LANES]
-            high = angles_ref[rows, 2 * LANES : 2 * LANES + 2 * coarse]
-            for b in range(coarse):
-                value = high[:, b : b + 1] * cos_lo - high[:, coarse + b : coarse + b + 1] * sin_lo
-                table_ref[h, local, b * LANES : (b + 1) * LANES] = value.astype(BF16)
-
-        loop(0, columns // 16, rows_step)
+        rows = lax.broadcasted_iota(jnp.int32, (phase_ref.shape[0], columns), 0)
+        pick = jnp.where(rows == pick_ref[h], 1.0, 0.0).astype(BF16)
+
+        def lon_step(t):
+            cells = pl.ds(pl.multiple_of(t * 512, 512), 512)
+            table_ref[h, :, cells] = lax.dot_general(
+                pick, phase_ref[:, cells], (((0,), (0,)), ((), ())), preferred_element_type=F32
+            ).astype(BF16)
+
+        loop(0, lon_cells // 512, lon_step)
 
     factor = 1.0 / math.sqrt(lon_cells)
     tile = 4 * rows_dev * 2
@@ -167,9 +164,6 @@
         recv[h, me] = sent[h, me]
 
     loop(0, chunks, forward_chunk)
-    save_table = pltpu.make_async_copy(table_ref, table_hbm, load_sem.at[1])
-    save_table.start()
-
     wide = 128
 
     def middle_chunk(h):
@@ -179,7 +173,7 @@
             cols = pl.ds(pl.multiple_of(t * wide, wide), wide)
             rows = recv[h, :, :, cols].astype(F32).reshape(lat_rows, wide).astype(BF16)
             value = lax.dot_general(
-                rows, place_ref[...], (((0,), (0,)), ((), ())), preferred_element_type=F32
+                rows, place_ref[...], (((0,), (1,)), ((), ())), preferred_element_type=F32
             )
             for b in range(blocks):
                 side[b, cols, :] = value[:, b * LANES : (b + 1) * LANES]
@@ -200,7 +194,7 @@
             leg_copy(g).wait()
             table = leg_buf[lax.rem(g, buffers)]
             result = jnp.dot(both, table, preferred_element_type=F32)
-            offsets = lax.broadcasted_iota(jnp.int32, (1, total), 1) - wave_ref[g]
+            offsets = lax.broadcasted_iota(jnp.int32, (1, total), 1) - wave_ref[me * slots + g]
             sign = jnp.where(offsets % 2 == 0, 1.0, -1.0).astype(F32)
             spec = jnp.where(offsets >= 0, result[:items] + sign * result[items:], 0.0)
 
@@ -228,53 +222,92 @@
             cols = pl.ds(pl.multiple_of(t * wide, wide), wide)
             value = jnp.concatenate([fold[b, cols, :] for b in range(blocks)], axis=1).astype(BF16)
             rows = lax.dot_general(
-                place_ref[...], value, (((1,), (1,)), ((), ())), preferred_element_type=F32
+                place_ref[...], value, (((0,), (1,)), ((), ())), preferred_element_type=F32
             )
             back[h, :, :, cols] = rows.reshape(owners, rows_dev, wide).astype(BF16)
 
         loop(0, lanes // wide, pack)
         loop(1, owners, lambda d: out_back(h, d).start())
-        own_back(h).start()
+        returned[h, me] = back[h, me]
 
     loop(0, chunks, middle_chunk)
     spec_copy(slots - 2).wait()
     spec_copy(slots - 1).wait()
-    save_table.wait()
+
+    scale = 1.0 / math.sqrt(owners * slots)
+    tiles = levels * rows_dev // tile
+
+    def smooth_copy(t):
+        rows = pl.ds(pl.multiple_of(t * tile, tile), tile)
+        return pltpu.make_async_copy(x_ref.at[rows], smooth_hbm.at[rows], smooth_sem.at[t])
+
+    def inverse_chunk(h):
+        loop(1, owners, lambda d: in_back(h, d).wait_recv())
+        for k in range(levels):
+            parts = [
+                returned[h, w, :, k * piece : (k + 1) * piece].astype(F32) for w in range(owners)
+            ]
+            y_ref[k * rows_dev : (k + 1) * rows_dev, :] = jnp.concatenate(parts, axis=1)
+
+        def dot_step(t):
+            rows = pl.ds(pl.multiple_of(t * tile, tile), tile)
+            term = jnp.dot(y_ref[rows, :].astype(BF16), table_ref[h], preferred_element_type=F32)
+
+            @pl.when(h == 0)
+            def _():
+                total_ref[rows, :] = term
+
+            @pl.when(jnp.logical_and(h > 0, h < chunks - 1))
+            def _():
+                total_ref[rows, :] += term
+
+            @pl.when(h == chunks - 1)
+            def _():
+                x_ref[rows, :] = ((total_ref[rows, :] + term) * scale).astype(BF16)
+                smooth_copy(t).start()
+
+        loop(0, tiles, dot_step)
+
+    loop(0, chunks, inverse_chunk)
 
     def finish(h):
         loop(1, owners, lambda d: out_copy(h, d).wait_send())
         loop(1, owners, lambda d: out_back(h, d).wait_send())
-        loop(1, owners, lambda d: in_back(h, d).wait_recv())
-        own_back(h).wait()
 
     loop(0, chunks, finish)
-
-
-def exchange(chunks, owners, rows_dev, mine, x, angles, place, table, spectrum):
+    loop(0, tiles, lambda t: smooth_copy(t).wait())
+
+
+def exchange(chunks, owners, rows_dev, waves, x, phases, picks, column, table, spectrum):
     slots, north, total = table.shape
     lon_cells = x.shape[1]
     levels = x.shape[0] // rows_dev
     chunk = slots // chunks
     lanes = 2 * levels * chunk
     columns = owners * 2 * chunk
-    blocks = place.shape[1] // LANES
+    lat_rows = owners * rows_dev
+    blocks = 2 * up(north, LANES) // LANES
+    tiles = levels // 8
     hbm = pl.BlockSpec(memory_space=pl.ANY)
     vmem = pl.BlockSpec(memory_space=pltpu.VMEM)
     block = (chunks, owners, rows_dev, lanes)
     sems = pltpu.SemaphoreType.DMA
     return pl.pallas_call(
         functools.partial(exchange_body, owners, chunks),
-        in_specs=[pl.BlockSpec(memory_space=pltpu.SMEM), hbm, vmem, vmem, hbm, vmem],
-        out_specs=[hbm, hbm, hbm],
+        in_specs=[pl.BlockSpec(memory_space=pltpu.SMEM), hbm, hbm, vmem, vmem, hbm, vmem],
+        out_specs=[hbm, hbm],
         out_shape=[
             jax.ShapeDtypeStruct((slots, 2 * levels, total), BF16),
-            jax.ShapeDtypeStruct(block, BF16),
-            jax.ShapeDtypeStruct((chunks, columns, lon_cells), BF16),
+            jax.ShapeDtypeStruct(x.shape, BF16),
         ],
         scratch_shapes=[
             pltpu.VMEM(x.shape, BF16),
+            pltpu.VMEM(phases.shape, BF16),
             pltpu.VMEM((chunks, columns, lon_cells), BF16),
             pltpu.VMEM((x.shape[0], columns), F32),
+            pltpu.VMEM(x.shape, F32),
+            pltpu.VMEM((blocks * LANES, lat_rows), BF16),
+            pltpu.VMEM(block, BF16),
             pltpu.VMEM(block, BF16),
             pltpu.VMEM(block, BF16),
             pltpu.VMEM(block, BF16),
@@ -289,7 +322,7 @@
             sems((2,)),
             sems((4,)),
             sems((2,)),
-            sems((chunks,)),
+            sems((tiles,)),
         ],
         compiler_params=params(collective_id=0, has_side_effects=True),
         cost_estimate=pl.CostEstimate(
@@ -298,43 +331,7 @@
             transcendentals=0,
         ),
         name="fourier_legendre_exchange",
-    )(mine, x, angles, place, table, spectrum)
-
-
-def inverse_body(rows_dev, group, piece, factor, returned_ref, table_ref, out_ref):
-    chunks, owners = returned_ref.shape[:2]
-    total = None
-    for h in range(chunks):
-        blocks = [returned_ref[h, w].astype(F32) for w in range(owners)]
-        rows = [
-            jnp.concatenate([b[:, k * piece : (k + 1) * piece] for b in blocks], axis=1)
-            for k in range(group)
-        ]
-        z = jnp.concatenate(rows, axis=0).astype(BF16)
-        term = jnp.dot(z, table_ref[h], preferred_element_type=F32)
-        total = term if total is None else total + term
-    out_ref[...] = (total * factor).astype(BF16)
-
-
-def inverse(returned, tables, waves_count):
-    chunks, owners, rows_dev, lanes = returned.shape
-    columns, lon_cells = tables.shape[1:]
-    piece = columns // owners
-    items = lanes // piece
-    group = LANES // math.gcd(piece, LANES)
-    body = functools.partial(inverse_body, rows_dev, group, piece, 1.0 / math.sqrt(waves_count))
-    return pl.pallas_call(
-        body,
-        grid=(items // group,),
-        in_specs=[
-            pl.BlockSpec((chunks, owners, rows_dev, group * piece), lambda g: (0, 0, 0, g)),
-            pl.BlockSpec(tables.shape, lambda g: (0, 0, 0)),
-        ],
-        out_specs=pl.BlockSpec((group * rows_dev, lon_cells), lambda g: (g, 0)),
-        out_shape=jax.ShapeDtypeStruct((items * rows_dev, lon_cells), BF16),
-        compiler_params=params(),
-        name="inverse_fourier",
-    )(returned, tables)
+    )(waves, x, phases, picks, column, table, spectrum)
 
 
 def kernels_fit(owners, items, rows_dev, slots, north, total, lon_cells):
@@ -347,7 +344,7 @@
         and items % 8 == 0
         and items % group == 0
         and total % LANES == 0
-        and lon_cells % (4 * LANES) == 0
+        and lon_cells % 512 == 0
         and owners * piece % 16 == 0
         and slots > 4
     )
@@ -358,18 +355,17 @@
     items, rows_dev, lon_cells = grid_grad.shape
     slots, total, north = legendre.shape
     waves = owner_waves.reshape(owners, slots)
-    mine = lax.dynamic_index_in_dim(waves, lax.axis_index("wave"), 0, keepdims=False)
     x = grid_grad.reshape(items * rows_dev, lon_cells)
     table = jnp.swapaxes(legendre, 1, 2)
     half = up(north, LANES)
-    column = jnp.where(lat_order < north, lat_order, lat_order - north + half)
-    place = (column[:, None] == lax.iota(jnp.int32, 2 * half)[None, :]).astype(BF16)
-    in_chunks = jnp.swapaxes(waves.reshape(owners, PARTS, slots // PARTS), 0, 1)
-    angles = angle_tables(in_chunks, lon_cells)
-    spec, returned, phases = exchange(
-        PARTS, owners, rows_dev, mine, x, angles, place, table, spectrum[None, :]
-    )
-    smoothed = inverse(returned, phases, owners * slots)
+    column = jnp.where(lat_order < north, lat_order, lat_order - north + half)[None, :]
+    chunk = slots // PARTS
+    in_chunks = jnp.swapaxes(waves.reshape(owners, PARTS, chunk), 0, 1)
+    picks = jnp.stack([in_chunks, in_chunks + owners * slots], axis=2).reshape(PARTS, 1, -1)
+    phases = jnp.asarray(phase_constants(owners * slots, lon_cells))
+    spec, smoothed = exchange(
+        PARTS, owners, rows_dev, owner_waves, x, phases, picks, column, table, spectrum[None, :]
+    )
     return (spec, smoothed.reshape(grid_grad.shape))
 
 

time: 198 us -> 181 us (0.914)
  Pallas kernels: 179 us -> 167 us
  other arithmetic: 11.3 us -> 0.72 us
  local copies, waits for them, and re-layouts: 6.57 us -> 12.8 us
    pallas_call x1 -> x0, Pallas kernels: 21.6 us -> none  [inverse(): pl.pallas_call(body, grid=(items // group,), in_specs=[pl.BlockSpec((chun...]
    pallas_call x1, Pallas kernels: 157 us -> 167 us  [exchange(): pl.pallas_call(functools.partial(exchange_body, owners, chunks), in_specs...]
    cos x1 -> x0, other arithmetic: 8.83 us -> none  [angle_tables(): return jnp.cos(ticks.astype(F32) * (2.0 * math.pi / lon_cells))]
    unnamed x3 -> x4, local copies, waits for them, and re-layouts: 2.79 us -> 9.35 us
where the time goes in v1:
time: 181 us
  Pallas kernels  167 us (92%)
  local copies, waits for them, and re-layouts  12.8 us (7%)
    pallas_call x1, Pallas kernels, exchange(): pl.pallas_call(functools.partial(exchange_body, owners, chunks), in_specs...  167 us
    unnamed x4, local copies, waits for them, and re-layouts  9.35 us

profile of v1, /device:TPU:15, one launch (start us, length us, event | category | flops | bytes accessed | tf_op | source)
XLA Modules:
  0.0 180.8 jit_solution(1635145003371674832)
XLA Ops:
  0.6 0.7 compare_select_fusion
  1.3 0.6 broadcast_in_dim.6.column_ref
  1.9 1.3 broadcast_in_dim.7.spectrum_ref
  3.2 0.8 reshape_reshape.3
  4.1 0.1 copy.9
  4.1 0.7 reshape.16.pick_ref
  4.9 166.5 %fourier_legendre_exchange.1 = (bf16[40,64,1280]{2,1,0:T(8,128)(2,1)}, bf16[1280,2560]{1,0:T(8,128)(2,1)}) custom-call(s32[640]{0:T(1024)} %wave_ref.1, bf16[1280,2560]{1,0:T(8,128)(2,1)} %bitcast.14, bf16[1280,2560]{1,0:T(8,128)(2,1)} %constant.10.clone.phase_hbm, s32[4,1,320]{2,1,0:T(1,128)} %reshape.16.pick_ref, s32[1,640]{1,0:T(1,128)} %broadcast_in_dim.6.column_ref, ...), custom_call_target="tpu_custom_call" | custom-call | flops 16777216000 | bytes 65536000 | tf_op jit(solution)/shard_map/fourier_legendre_exchange/pallas_call | solution.py:295
  171.4 0.0 copy-start
  171.4 6.6 %copy.13 = bf16[40,64,1280]{2,1,0:T(8,128)(2,1)} copy(bf16[40,64,1280]{2,1,0:T(8,128)(2,1)} %get-tuple-element.8) | data formatting | bytes 13107200
  178.0 0.0 copy-done
  178.0 2.8 %copy.14 = bf16[32,40,2560]{2,1,0:T(8,128)(2,1)} copy(bf16[32,40,2560]{2,1,0:T(8,128)(2,1)S(1)} %bitcast.11) | data formatting | bytes 13107200
  (2 shorter events, 0.0 us)
Async XLA Ops:
  171.4 6.6 %copy-start = (bf16[1280,2560]{1,0:T(8,128)(2,1)S(1)}, bf16[1280,2560]{1,0:T(8,128)(2,1)}, u32[]{:S(2)}) copy-start(bf16[1280,2560]{1,0:T(8,128)(2,1)} %get-tuple-element.5) | copy-start | bytes 19660804

commit v2 on v1

--- a/solution.py
+++ b/solution.py
@@ -32,7 +32,7 @@
 
 
 def exchange_body(
-    owners, chunks, wave_ref, x_hbm, phase_hbm, pick_ref, column_ref, leg_hbm, spectrum_ref,
+    owners, chunks, wave_ref, x_hbm, phase_hbm, pick_ref, lat_ref, leg_hbm, spectrum_ref,
     spec_hbm, smooth_hbm,
     x_ref, phase_ref, table_ref, y_ref, total_ref, place_ref,
     sent, recv, back, returned, side, fold, leg_buf, spec_buf,
@@ -105,6 +105,11 @@
 
         lax.fori_loop(low, high, body, 0)
 
+    middle = owners // 2
+
+    def far_first(i):
+        return middle + (i // 2) * (1 - 2 * (i % 2))
+
     barrier = pltpu.get_barrier_semaphore()
 
     def greet(d):
@@ -113,11 +118,10 @@
         )
 
     loop(1, owners, greet)
-    for g in range(buffers - 1):
-        leg_copy(g).start()
-
+    lat = lat_ref[...].reshape(1, lat_rows)
+    column = jnp.where(lat < north, lat, lat - north + half * LANES)
     place_ref[...] = jnp.where(
-        lax.broadcasted_iota(jnp.int32, place_ref.shape, 0) == column_ref[...], 1.0, 0.0
+        lax.broadcasted_iota(jnp.int32, place_ref.shape, 0) == column, 1.0, 0.0
     ).astype(BF16)
     load_phase.wait()
 
@@ -160,10 +164,13 @@
         def _():
             pl.semaphore_wait(barrier, owners - 1)
 
-        loop(1, owners, lambda d: out_copy(h, d).start())
+        loop(1, owners, lambda i: out_copy(h, far_first(i)).start())
         recv[h, me] = sent[h, me]
 
     loop(0, chunks, forward_chunk)
+    for g in range(buffers - 1):
+        leg_copy(g).start()
+
     wide = 128
 
     def middle_chunk(h):
@@ -204,7 +211,7 @@
 
             spec_buf[lax.rem(g, 2)] = spec.astype(BF16)
             spec_copy(g).start()
-            filtered = (spec * spectrum_ref[...]).astype(BF16).astype(F32)
+            filtered = (spec * spectrum_ref[...].reshape(1, total)).astype(BF16).astype(F32)
             second = jnp.concatenate([filtered, filtered * sign], axis=0).astype(BF16)
             folded = lax.dot_general(second, table, (((1,), (1,)), ((), ())), preferred_element_type=F32)
             folded = folded.astype(BF16).astype(F32)
@@ -227,7 +234,7 @@
             back[h, :, :, cols] = rows.reshape(owners, rows_dev, wide).astype(BF16)
 
         loop(0, lanes // wide, pack)
-        loop(1, owners, lambda d: out_back(h, d).start())
+        loop(1, owners, lambda i: out_back(h, far_first(i)).start())
         returned[h, me] = back[h, me]
 
     loop(0, chunks, middle_chunk)
@@ -347,6 +354,7 @@
         and lon_cells % 512 == 0
         and owners * piece % 16 == 0
         and slots > 4
+        and owners % 2 == 0
     )
 
 
@@ -357,14 +365,12 @@
     waves = owner_waves.reshape(owners, slots)
     x = grid_grad.reshape(items * rows_dev, lon_cells)
     table = jnp.swapaxes(legendre, 1, 2)
-    half = up(north, LANES)
-    column = jnp.where(lat_order < north, lat_order, lat_order - north + half)[None, :]
     chunk = slots // PARTS
     in_chunks = jnp.swapaxes(waves.reshape(owners, PARTS, chunk), 0, 1)
     picks = jnp.stack([in_chunks, in_chunks + owners * slots], axis=2).reshape(PARTS, 1, -1)
     phases = jnp.asarray(phase_constants(owners * slots, lon_cells))
     spec, smoothed = exchange(
-        PARTS, owners, rows_dev, owner_waves, x, phases, picks, column, table, spectrum[None, :]
+        PARTS, owners, rows_dev, owner_waves, x, phases, picks, lat_order, table, spectrum
     )
     return (spec, smoothed.reshape(grid_grad.shape))
 

time: 181 us -> 180 us (level); the launches traced: 181 us -> 178 us
    broadcast_in_dim x2 -> x0, local copies, waits for them, and re-layouts: 1.89 us -> none  [the longest x1 1.29 us: local_kernels(): spectrum[None, :]]
where the time goes in v2:
time: 180 us; the launch traced here: 178 us
  Pallas kernels  166 us (92%)
  local copies, waits for them, and re-layouts  11 us (6%)
    pallas_call x1, Pallas kernels, exchange(): pl.pallas_call(functools.partial(exchange_body, owners, chunks), in_specs...  166 us
    unnamed x4, local copies, waits for them, and re-layouts  9.35 us

profile of v2, /device:TPU:15, one launch (start us, length us, event | category | flops | bytes accessed | tf_op | source)
XLA Modules:
  0.0 177.8 jit_solution(10611065661206086618)
XLA Ops:
  0.6 0.8 reshape_reshape.3
  1.5 0.1 copy.9
  1.6 0.7 reshape.16.pick_ref
  2.3 166.2 %fourier_legendre_exchange.1 = (bf16[40,64,1280]{2,1,0:T(8,128)(2,1)}, bf16[1280,2560]{1,0:T(8,128)(2,1)}) custom-call(s32[640]{0:T(1024)} %wave_ref.1, bf16[1280,2560]{1,0:T(8,128)(2,1)} %bitcast.14, bf16[1280,2560]{1,0:T(8,128)(2,1)} %constant.4.clone.phase_hbm, s32[4,1,320]{2,1,0:T(1,128)} %reshape.16.pick_ref, s32[640]{0:T(1024)} %lat_ref.1, ...), custom_call_target="tpu_custom_call" | custom-call | flops 16777216000 | bytes 65536000 | tf_op jit(solution)/shard_map/fourier_legendre_exchange/pallas_call | solution.py:302
  168.5 0.0 copy-start
  168.5 6.6 %copy.13 = bf16[40,64,1280]{2,1,0:T(8,128)(2,1)} copy(bf16[40,64,1280]{2,1,0:T(8,128)(2,1)} %get-tuple-element.8) | data formatting | bytes 13107200
  175.0 0.0 copy-done
  175.0 2.8 %copy.14 = bf16[32,40,2560]{2,1,0:T(8,128)(2,1)} copy(bf16[32,40,2560]{2,1,0:T(8,128)(2,1)S(1)} %bitcast.11) | data formatting | bytes 13107200
  (2 shorter events, 0.0 us)
Async XLA Ops:
  168.5 6.6 %copy-start = (bf16[1280,2560]{1,0:T(8,128)(2,1)S(1)}, bf16[1280,2560]{1,0:T(8,128)(2,1)}, u32[]{:S(2)}) copy-start(bf16[1280,2560]{1,0:T(8,128)(2,1)} %get-tuple-element.5) | copy-start | bytes 19660804

commit v3 on v2

--- a/solution.py
+++ b/solution.py
@@ -105,11 +105,6 @@
 
         lax.fori_loop(low, high, body, 0)
 
-    middle = owners // 2
-
-    def far_first(i):
-        return middle + (i // 2) * (1 - 2 * (i % 2))
-
     barrier = pltpu.get_barrier_semaphore()
 
     def greet(d):
@@ -164,7 +159,7 @@
         def _():
             pl.semaphore_wait(barrier, owners - 1)
 
-        loop(1, owners, lambda i: out_copy(h, far_first(i)).start())
+        loop(1, owners, lambda d: out_copy(h, d).start())
         recv[h, me] = sent[h, me]
 
     loop(0, chunks, forward_chunk)
@@ -234,7 +229,7 @@
             back[h, :, :, cols] = rows.reshape(owners, rows_dev, wide).astype(BF16)
 
         loop(0, lanes // wide, pack)
-        loop(1, owners, lambda i: out_back(h, far_first(i)).start())
+        loop(1, owners, lambda d: out_back(h, d).start())
         returned[h, me] = back[h, me]
 
     loop(0, chunks, middle_chunk)
@@ -354,7 +349,6 @@
         and lon_cells % 512 == 0
         and owners * piece % 16 == 0
         and slots > 4
-        and owners % 2 == 0
     )
 
 

time: 180 us -> 178 us (0.989); the launches traced: 178 us -> 178 us
  no operation moved by 1% of the time
where the time goes in v3:
time: 178 us
  Pallas kernels  167 us (94%)
  local copies, waits for them, and re-layouts  11 us (6%)
    pallas_call x1, Pallas kernels, exchange(): pl.pallas_call(functools.partial(exchange_body, owners, chunks), in_specs...  167 us
    unnamed x4, local copies, waits for them, and re-layouts  9.35 us

profile of v3, /device:TPU:15, one launch (start us, length us, event | category | flops | bytes accessed | tf_op | source)
XLA Modules:
  0.0 178.2 jit_solution(96253878333985068)
XLA Ops:
  0.6 0.8 reshape_reshape.3
  1.5 0.1 copy.9
  1.6 0.7 reshape.16.pick_ref
  2.3 166.5 %fourier_legendre_exchange.1 = (bf16[40,64,1280]{2,1,0:T(8,128)(2,1)}, bf16[1280,2560]{1,0:T(8,128)(2,1)}) custom-call(s32[640]{0:T(1024)} %wave_ref.1, bf16[1280,2560]{1,0:T(8,128)(2,1)} %bitcast.14, bf16[1280,2560]{1,0:T(8,128)(2,1)} %constant.4.clone.phase_hbm, s32[4,1,320]{2,1,0:T(1,128)} %reshape.16.pick_ref, s32[640]{0:T(1024)} %lat_ref.1, ...), custom_call_target="tpu_custom_call" | custom-call | flops 16777216000 | bytes 65536000 | tf_op jit(solution)/shard_map/fourier_legendre_exchange/pallas_call | solution.py:297
  168.8 0.0 copy-start
  168.8 6.6 %copy.13 = bf16[40,64,1280]{2,1,0:T(8,128)(2,1)} copy(bf16[40,64,1280]{2,1,0:T(8,128)(2,1)} %get-tuple-element.8) | data formatting | bytes 13107200
  175.4 0.0 copy-done
  175.4 2.8 %copy.14 = bf16[32,40,2560]{2,1,0:T(8,128)(2,1)} copy(bf16[32,40,2560]{2,1,0:T(8,128)(2,1)S(1)} %bitcast.11) | data formatting | bytes 13107200
  (2 shorter events, 0.0 us)
Async XLA Ops:
  168.8 6.6 %copy-start = (bf16[1280,2560]{1,0:T(8,128)(2,1)S(1)}, bf16[1280,2560]{1,0:T(8,128)(2,1)}, u32[]{:S(2)}) copy-start(bf16[1280,2560]{1,0:T(8,128)(2,1)} %get-tuple-element.5) | copy-start | bytes 19660804
